TPU v7x, 512 devices: a whole 4x8x8 slice. The times are simulated.
512 devices in a mesh: row: 32 (over y, x), col: 16 (over z, core).
Axes of the slice: x: 4, y: 8, z: 8, core: 2. Of those that a mesh axis runs over, the one named last changes fastest.
Arguments:
- activations: bfloat16 [576, 8192], P('row', 'col'), may hold values from -6 to 6
- gate_matrix: bfloat16 [8192, 28672], P('col', 'row'), may hold values from -0.0625 to 0.0625
- up_matrix: bfloat16 [8192, 28672], P('col', 'row'), may hold values from -0.0625 to 0.0625
- down_matrix: bfloat16 [28672, 8192], P('row', 'col'), may hold values from -0.03125 to 0.03125
Outputs:
- layer_out: bfloat16 [576, 8192], P('row', 'col')
All inputs are finite; a program needn't handle non-finite values.
Results may differ from a plain program's by a relative error of at most 0.0049.
Values may be sent and summed in bfloat16 or wider, within the bound.
No kernel may reach another device: no remote copies, remote signals or barrier semaphores. Data moves between devices by JAX's collectives and lax.ppermute only.
A program may use at most 64 MiB of HBM per device.

v0:
```python
import jax
import jax.numpy as jnp
from jax import lax
from jax.sharding import PartitionSpec as P


def activate(summed, hidden_width):
    gate_part = summed[:, :hidden_width]
    up_part = summed[:, hidden_width:]
    return (jax.nn.silu(gate_part) * up_part).astype(jnp.bfloat16)


def shards(activations, gate_matrix, up_matrix, down_matrix):
    gathered = lax.all_gather(activations, "row", axis=0, tiled=True)
    hidden_width = gate_matrix.shape[1]
    gate_term = jnp.dot(gathered, gate_matrix, preferred_element_type=jnp.float32)
    up_term = jnp.dot(gathered, up_matrix, preferred_element_type=jnp.float32)
    summed = lax.psum(jnp.concatenate([gate_term, up_term], axis=1), "col")
    hidden = activate(summed, hidden_width)
    partial_out = jnp.dot(hidden, down_matrix, preferred_element_type=jnp.float32)
    result = lax.psum_scatter(partial_out, "row", scatter_dimension=0, tiled=True)
    return result.astype(jnp.bfloat16)


def solution(mesh):
    placed = (P("row", "col"), P("col", "row"), P("col", "row"), P("row", "col"))
    return jax.shard_map(
        shards, mesh=mesh, in_specs=placed, out_specs=P("row", "col"), check_vma=False
    )
```

profile of v0, /device:TPU:14, one launch (start us, length us, event | category | flops | bytes accessed | tf_op | source)
XLA Modules:
  0.0 315.8 jit_solution(8600206868353178816)
XLA Ops:
  6.5 50.4 %all-gather = bf16[32,18,512]{2,1,0:T(8,128)(2,1)S(1)} all-gather(bf16[1,18,512]{2,1,0:T(8,128)(2,1)} %bitcast.9), channel_id=1, replica_groups=mesh['row'=32,'col'=16] {'row'}, dimensions={0}, use_global_device_ids=true | all-gather | bytes 608256 | tf_op jit(solution)/shard_map/all_gather | solution.py:14
  57.0 0.2 reshape.1
  57.2 0.0 copy-start.1
  57.2 0.8 fusion.6
  58.0 0.4 copy-done.1
  58.4 0.8 fusion.7
  59.1 2.3 pad_maximum_fusion
  61.4 0.0 all-reduce.4.cloned.1.call-update
  61.4 129.4 %all-reduce.4.cloned.1.call-done = f32[576,1792]{1,0:T(8,128)} async-done(((f32[576,1792]{1,0:T(8,128)}), f32[576,1792]{1,0:T(8,128)}) %all-reduce.4.cloned.1.call-update) | async-done | bytes 4128784 | tf_op jit(solution)/shard_map/psum | solution.py:18
  190.8 3.0 fusion.2
  193.8 72.6 %fusion = f32[24,512]{1,0:T(8,128)S(1)} fusion(f32[576,512]{1,0:T(8,128)S(1)} %fusion.2), kind=kCustom, calls=%all-reduce-scatter | all-reduce-scatter fusion | flops 393217 | bytes 1230848
  266.4 4.2 %collective-permute-start = (bf16[24,512]{1,0:T(8,128)(2,1)S(1)}, bf16[24,512]{1,0:T(8,128)(2,1)S(1)}, u32[]{:S(2)}, u32[]{:S(2)}) collective-permute-start(bf16[24,512]{1,0:T(8,128)(2,1)S(1)} %convert.14), channel_id=1, source_target_pairs={{0,16},{16,32},{32,48},{48,64},{64,80},{80,96},{96,112},{112,128},... | collective-permute-start | bytes 73736
  270.6 5.0 %collective-permute-start.1 = (bf16[24,512]{1,0:T(8,128)(2,1)S(1)}, bf16[24,512]{1,0:T(8,128)(2,1)S(1)}, u32[]{:S(2)}, u32[]{:S(2)}) collective-permute-start(bf16[24,512]{1,0:T(8,128)(2,1)S(1)} %convert.14), channel_id=1, source_target_pairs={{0,32},{16,48},{32,64},{48,80},{64,96},{80,112},{96,128},{112,144}... | collective-permute-start | bytes 73736
  275.6 12.3 %collective-permute-start.7 = (bf16[18,512]{1,0:T(8,128)(2,1)S(1)}, bf16[18,512]{1,0:T(8,128)(2,1)S(1)}, u32[]{:S(2)}, u32[]{:S(2)}) collective-permute-start(bf16[18,512]{1,0:T(8,128)(2,1)S(1)} %slice.10), channel_id=1, source_target_pairs={{0,128},{16,144},{32,160},{48,176},{64,192},{80,208},{96,224},{112... | collective-permute-start | bytes 55304
  287.9 1.9 collective-permute-start.2
  289.8 3.1 collective-permute-start.3
  292.9 3.4 %collective-permute-start.4 = (bf16[24,512]{1,0:T(8,128)(2,1)S(1)}, bf16[24,512]{1,0:T(8,128)(2,1)S(1)}, u32[]{:S(2)}, u32[]{:S(2)}) collective-permute-start(bf16[24,512]{1,0:T(8,128)(2,1)S(1)} %convert.14), channel_id=1, source_target_pairs={{0,80},{16,96},{32,112},{48,128},{64,144},{80,160},{96,176},{112,1... | collective-permute-start | bytes 73736
  296.3 3.0 collective-permute-start.5
  299.4 1.9 collective-permute-start.6
  301.3 1.3 dynamic-slice.4
  303.3 1.2 collective-permute-done.5
  304.5 2.8 collective-permute-done.6
  307.2 1.1 concatenate.4
  308.3 0.6 dynamic-slice_convert_fusion
  (13 shorter events, 0.0 us)
Async XLA Ops:
  6.5 50.6 %copy-start = (bf16[512,896]{1,0:T(8,128)(2,1)S(1)}, bf16[512,896]{1,0:T(8,128)(2,1)}, u32[]{:S(2)}) copy-start(bf16[512,896]{1,0:T(8,128)(2,1)} %param.5) | copy-start | bytes 2752516
  6.5 184.2 %all-reduce.4.cloned.1.call-start = ((), (), s32[]{:S(2)}) async-start(), calls=%async_computation | async-start | bytes 8257536 | tf_op jit(solution)/shard_map/psum | solution.py:18
  57.2 1.2 copy-start.1
  61.4 129.4 %copy-start.2 = (bf16[896,512]{1,0:T(8,128)(2,1)S(1)}, bf16[896,512]{1,0:T(8,128)(2,1)}, u32[]{:S(2)}) copy-start(bf16[896,512]{1,0:T(8,128)(2,1)} %param.7) | copy-start | bytes 2752516
  266.4 29.9 %collective-permute-start = (bf16[24,512]{1,0:T(8,128)(2,1)S(1)}, bf16[24,512]{1,0:T(8,128)(2,1)S(1)}, u32[]{:S(2)}, u32[]{:S(2)}) collective-permute-start(bf16[24,512]{1,0:T(8,128)(2,1)S(1)} %convert.14), channel_id=1, source_target_pairs={{0,16},{16,32},{32,48},{48,64},{64,80},{80,96},{96,112},{112,128},... | collective-permute-start | bytes 73736
  270.6 28.8 %collective-permute-start.1 = (bf16[24,512]{1,0:T(8,128)(2,1)S(1)}, bf16[24,512]{1,0:T(8,128)(2,1)S(1)}, u32[]{:S(2)}, u32[]{:S(2)}) collective-permute-start(bf16[24,512]{1,0:T(8,128)(2,1)S(1)} %convert.14), channel_id=1, source_target_pairs={{0,32},{16,48},{32,64},{48,80},{64,96},{80,112},{96,128},{112,144}... | collective-permute-start | bytes 73736
  275.6 17.3 %collective-permute-start.7 = (bf16[18,512]{1,0:T(8,128)(2,1)S(1)}, bf16[18,512]{1,0:T(8,128)(2,1)S(1)}, u32[]{:S(2)}, u32[]{:S(2)}) collective-permute-start(bf16[18,512]{1,0:T(8,128)(2,1)S(1)} %slice.10), channel_id=1, source_target_pairs={{0,128},{16,144},{32,160},{48,176},{64,192},{80,208},{96,224},{112... | collective-permute-start | bytes 55304
  287.9 15.4 %collective-permute-start.2 = (bf16[24,512]{1,0:T(8,128)(2,1)S(1)}, bf16[24,512]{1,0:T(8,128)(2,1)S(1)}, u32[]{:S(2)}, u32[]{:S(2)}) collective-permute-start(bf16[24,512]{1,0:T(8,128)(2,1)S(1)} %convert.14), channel_id=1, source_target_pairs={{0,48},{16,64},{32,80},{48,96},{64,112},{80,128},{96,144},{112,160... | collective-permute-start | bytes 73736
  289.8 13.5 %collective-permute-start.3 = (bf16[24,512]{1,0:T(8,128)(2,1)S(1)}, bf16[24,512]{1,0:T(8,128)(2,1)S(1)}, u32[]{:S(2)}, u32[]{:S(2)}) collective-permute-start(bf16[24,512]{1,0:T(8,128)(2,1)S(1)} %convert.14), channel_id=1, source_target_pairs={{0,64},{16,80},{32,96},{48,112},{64,128},{80,144},{96,160},{112,17... | collective-permute-start | bytes 73736
  292.9 10.4 %collective-permute-start.4 = (bf16[24,512]{1,0:T(8,128)(2,1)S(1)}, bf16[24,512]{1,0:T(8,128)(2,1)S(1)}, u32[]{:S(2)}, u32[]{:S(2)}) collective-permute-start(bf16[24,512]{1,0:T(8,128)(2,1)S(1)} %convert.14), channel_id=1, source_target_pairs={{0,80},{16,96},{32,112},{48,128},{64,144},{80,160},{96,176},{112,1... | collective-permute-start | bytes 73736
  296.3 8.1 %collective-permute-start.5 = (bf16[24,512]{1,0:T(8,128)(2,1)S(1)}, bf16[24,512]{1,0:T(8,128)(2,1)S(1)}, u32[]{:S(2)}, u32[]{:S(2)}) collective-permute-start(bf16[24,512]{1,0:T(8,128)(2,1)S(1)} %convert.14), channel_id=1, source_target_pairs={{0,96},{16,112},{32,128},{48,144},{64,160},{80,176},{96,192},{112,... | collective-permute-start | bytes 73736
  299.4 7.8 %collective-permute-start.6 = (bf16[24,512]{1,0:T(8,128)(2,1)S(1)}, bf16[24,512]{1,0:T(8,128)(2,1)S(1)}, u32[]{:S(2)}, u32[]{:S(2)}) collective-permute-start(bf16[24,512]{1,0:T(8,128)(2,1)S(1)} %convert.14), channel_id=1, source_target_pairs={{0,112},{16,128},{32,144},{48,160},{64,176},{80,192},{96,208},{112... | collective-permute-start | bytes 73736
Sparse Core Ops, SparseCore 0:
  61.5 129.1 all-reduce.3
where the time goes:
time: 316 us
  waiting for transfers between devices  133 us (42%)
  blocking collectives  123 us (39%)
  starting transfers between devices  34.8 us (11%)
  between operations  14.2 us (4%)
  matrix products  4.54 us (1%)
  local copies, waits for them, and re-layouts  3.62 us (1%)
    psum x1, waiting for transfers between devices, shards(): summed = lax.psum(jnp.concatenate([gate_term, up_term], axis=1), 'col')  129 us
    unnamed x1, blocking collectives  72.6 us
    all_gather x1, blocking collectives, shards(): gathered = lax.all_gather(activations, 'row', axis=0, tiled=True)  50.4 us
    unnamed x8, starting transfers between devices  34.8 us
  transfers between devices with their start and end apart: 9, of which 3 were waited for; matrix products, arithmetic and copies ran while one was open for 0% of the time, Pallas kernels for 0%

commit v1 on v0

--- a/solution.py
+++ b/solution.py
@@ -11,7 +11,12 @@
 
 
 def shards(activations, gate_matrix, up_matrix, down_matrix):
-    gathered = lax.all_gather(activations, "row", axis=0, tiled=True)
+    gathered = jnp.concatenate(
+        jax.lax.all_to_all(
+            jnp.stack(tuple((activations for _ in range(jax.lax.axis_size("row")))), 0), "row", 0, 0
+        ),
+        0,
+    )
     hidden_width = gate_matrix.shape[1]
     gate_term = jnp.dot(gathered, gate_matrix, preferred_element_type=jnp.float32)
     up_term = jnp.dot(gathered, up_matrix, preferred_element_type=jnp.float32)

time: 316 us -> 297 us (0.940)
  blocking collectives: 123 us -> 104 us
    all_gather x1 -> x0, blocking collectives: 50.4 us -> none  [shards(): gathered = lax.all_gather(activations, 'row', axis=0, tiled=True)]
    all_to_all x0 -> x1, blocking collectives: none -> 31.5 us  [shards(): jax.lax.all_to_all(jnp.stack(tuple((activations for _ in range(jax.lax.ax...]
where the time goes in v1:
time: 297 us
  waiting for transfers between devices  132 us (44%)
  blocking collectives  104 us (35%)
  starting transfers between devices  34.9 us (12%)
  between operations  14.2 us (5%)
  matrix products  4.54 us (2%)
  local copies, waits for them, and re-layouts  4.49 us (2%)
    psum x1, waiting for transfers between devices, shards(): summed = lax.psum(jnp.concatenate([gate_term, up_term], axis=1), 'col')  128 us
    unnamed x1, blocking collectives  72.5 us
    unnamed x8, starting transfers between devices  34.9 us
    all_to_all x1, blocking collectives, shards(): jax.lax.all_to_all(jnp.stack(tuple((activations for _ in range(jax.lax.ax...  31.5 us
  transfers between devices with their start and end apart: 9, of which 3 were waited for; matrix products, arithmetic and copies ran while one was open for 0% of the time, Pallas kernels for 0%

profile of v1, /device:TPU:14, one launch (start us, length us, event | category | flops | bytes accessed | tf_op | source)
XLA Modules:
  0.0 296.8 jit_solution(8170650973556186119)
XLA Ops:
  6.5 0.9 stack.2
  7.4 31.5 %all_to_all.5 = bf16[32,18,512]{2,1,0:T(8,128)(2,1)S(1)} all-to-all(bf16[32,18,512]{2,1,0:T(8,128)(2,1)S(1)} %stack.2), channel_id=1, replica_groups=mesh['row'=32,'col'=16] {'row'}, dimensions={0} | all-to-all | bytes 1179648 | tf_op jit(solution)/shard_map/all_to_all | solution.py:15
  38.9 0.2 reshape.5
  39.1 0.8 fusion.6
  39.9 0.4 copy-done.1
  40.2 0.8 fusion.7
  41.0 2.3 pad_maximum_fusion
  43.3 0.0 all-reduce.4.cloned.1.call-update
  43.3 128.4 %all-reduce.4.cloned.1.call-done = f32[576,1792]{1,0:T(8,128)} async-done(((f32[576,1792]{1,0:T(8,128)}), f32[576,1792]{1,0:T(8,128)}) %all-reduce.4.cloned.1.call-update) | async-done | bytes 4128784 | tf_op jit(solution)/shard_map/psum | solution.py:23
  171.7 3.0 %fusion.2 = f32[576,512]{1,0:T(8,128)S(1)} fusion(bf16[896,512]{1,0:T(8,128)(2,1)S(1)} %copy-done.2, f32[576,1792]{1,0:T(8,128)} %all-reduce.4.cloned.1.call-done), kind=kOutput, calls=%fused_computation.3 | convolution fusion | flops 531578880 | bytes 6225920 | tf_op jit(solution)/shard_map/dot_general | solution.py:25
  174.7 72.5 %fusion = f32[24,512]{1,0:T(8,128)S(1)} fusion(f32[576,512]{1,0:T(8,128)S(1)} %fusion.2), kind=kCustom, calls=%all-reduce-scatter | all-reduce-scatter fusion | flops 393217 | bytes 1230848
  247.3 4.2 %collective-permute-start = (bf16[24,512]{1,0:T(8,128)(2,1)S(1)}, bf16[24,512]{1,0:T(8,128)(2,1)S(1)}, u32[]{:S(2)}, u32[]{:S(2)}) collective-permute-start(bf16[24,512]{1,0:T(8,128)(2,1)S(1)} %convert.14), channel_id=1, source_target_pairs={{0,16},{16,32},{32,48},{48,64},{64,80},{80,96},{96,112},{112,128},... | collective-permute-start | bytes 73736
  251.5 5.0 %collective-permute-start.1 = (bf16[24,512]{1,0:T(8,128)(2,1)S(1)}, bf16[24,512]{1,0:T(8,128)(2,1)S(1)}, u32[]{:S(2)}, u32[]{:S(2)}) collective-permute-start(bf16[24,512]{1,0:T(8,128)(2,1)S(1)} %convert.14), channel_id=1, source_target_pairs={{0,32},{16,48},{32,64},{48,80},{64,96},{80,112},{96,128},{112,144}... | collective-permute-start | bytes 73736
  256.5 12.3 %collective-permute-start.7 = (bf16[18,512]{1,0:T(8,128)(2,1)S(1)}, bf16[18,512]{1,0:T(8,128)(2,1)S(1)}, u32[]{:S(2)}, u32[]{:S(2)}) collective-permute-start(bf16[18,512]{1,0:T(8,128)(2,1)S(1)} %slice.10), channel_id=1, source_target_pairs={{0,128},{16,144},{32,160},{48,176},{64,192},{80,208},{96,224},{112... | collective-permute-start | bytes 55304
  268.8 1.9 collective-permute-start.2
  270.8 3.1 %collective-permute-start.3 = (bf16[24,512]{1,0:T(8,128)(2,1)S(1)}, bf16[24,512]{1,0:T(8,128)(2,1)S(1)}, u32[]{:S(2)}, u32[]{:S(2)}) collective-permute-start(bf16[24,512]{1,0:T(8,128)(2,1)S(1)} %convert.14), channel_id=1, source_target_pairs={{0,64},{16,80},{32,96},{48,112},{64,128},{80,144},{96,160},{112,17... | collective-permute-start | bytes 73736
  273.8 3.4 %collective-permute-start.4 = (bf16[24,512]{1,0:T(8,128)(2,1)S(1)}, bf16[24,512]{1,0:T(8,128)(2,1)S(1)}, u32[]{:S(2)}, u32[]{:S(2)}) collective-permute-start(bf16[24,512]{1,0:T(8,128)(2,1)S(1)} %convert.14), channel_id=1, source_target_pairs={{0,80},{16,96},{32,112},{48,128},{64,144},{80,160},{96,176},{112,1... | collective-permute-start | bytes 73736
  277.3 3.0 %collective-permute-start.5 = (bf16[24,512]{1,0:T(8,128)(2,1)S(1)}, bf16[24,512]{1,0:T(8,128)(2,1)S(1)}, u32[]{:S(2)}, u32[]{:S(2)}) collective-permute-start(bf16[24,512]{1,0:T(8,128)(2,1)S(1)} %convert.14), channel_id=1, source_target_pairs={{0,96},{16,112},{32,128},{48,144},{64,160},{80,176},{96,192},{112,... | collective-permute-start | bytes 73736
  280.3 1.9 collective-permute-start.6
  282.3 1.3 dynamic-slice.4
  284.2 1.2 collective-permute-done.5
  285.4 2.8 collective-permute-done.6
  288.2 1.1 concatenate.4
  289.3 0.6 dynamic-slice_convert_fusion
  (14 shorter events, 0.0 us)
Async XLA Ops:
  6.5 32.5 %copy-start = (bf16[512,896]{1,0:T(8,128)(2,1)S(1)}, bf16[512,896]{1,0:T(8,128)(2,1)}, u32[]{:S(2)}) copy-start(bf16[512,896]{1,0:T(8,128)(2,1)} %param.5) | copy-start | bytes 2752516
  6.5 165.2 %all-reduce.4.cloned.1.call-start = ((), (), s32[]{:S(2)}) async-start(), calls=%async_computation.1 | async-start | bytes 8257536 | tf_op jit(solution)/shard_map/psum | solution.py:23
  39.1 1.2 copy-start.1
  43.3 128.5 %copy-start.2 = (bf16[896,512]{1,0:T(8,128)(2,1)S(1)}, bf16[896,512]{1,0:T(8,128)(2,1)}, u32[]{:S(2)}) copy-start(bf16[896,512]{1,0:T(8,128)(2,1)} %param.7) | copy-start | bytes 2752516
  247.3 30.0 %collective-permute-start = (bf16[24,512]{1,0:T(8,128)(2,1)S(1)}, bf16[24,512]{1,0:T(8,128)(2,1)S(1)}, u32[]{:S(2)}, u32[]{:S(2)}) collective-permute-start(bf16[24,512]{1,0:T(8,128)(2,1)S(1)} %convert.14), channel_id=1, source_target_pairs={{0,16},{16,32},{32,48},{48,64},{64,80},{80,96},{96,112},{112,128},... | collective-permute-start | bytes 73736
  251.5 28.8 %collective-permute-start.1 = (bf16[24,512]{1,0:T(8,128)(2,1)S(1)}, bf16[24,512]{1,0:T(8,128)(2,1)S(1)}, u32[]{:S(2)}, u32[]{:S(2)}) collective-permute-start(bf16[24,512]{1,0:T(8,128)(2,1)S(1)} %convert.14), channel_id=1, source_target_pairs={{0,32},{16,48},{32,64},{48,80},{64,96},{80,112},{96,128},{112,144}... | collective-permute-start | bytes 73736
  256.5 17.3 %collective-permute-start.7 = (bf16[18,512]{1,0:T(8,128)(2,1)S(1)}, bf16[18,512]{1,0:T(8,128)(2,1)S(1)}, u32[]{:S(2)}, u32[]{:S(2)}) collective-permute-start(bf16[18,512]{1,0:T(8,128)(2,1)S(1)} %slice.10), channel_id=1, source_target_pairs={{0,128},{16,144},{32,160},{48,176},{64,192},{80,208},{96,224},{112... | collective-permute-start | bytes 55304
  268.8 15.4 %collective-permute-start.2 = (bf16[24,512]{1,0:T(8,128)(2,1)S(1)}, bf16[24,512]{1,0:T(8,128)(2,1)S(1)}, u32[]{:S(2)}, u32[]{:S(2)}) collective-permute-start(bf16[24,512]{1,0:T(8,128)(2,1)S(1)} %convert.14), channel_id=1, source_target_pairs={{0,48},{16,64},{32,80},{48,96},{64,112},{80,128},{96,144},{112,160... | collective-permute-start | bytes 73736
  270.8 13.5 %collective-permute-start.3 = (bf16[24,512]{1,0:T(8,128)(2,1)S(1)}, bf16[24,512]{1,0:T(8,128)(2,1)S(1)}, u32[]{:S(2)}, u32[]{:S(2)}) collective-permute-start(bf16[24,512]{1,0:T(8,128)(2,1)S(1)} %convert.14), channel_id=1, source_target_pairs={{0,64},{16,80},{32,96},{48,112},{64,128},{80,144},{96,160},{112,17... | collective-permute-start | bytes 73736
  273.8 10.4 %collective-permute-start.4 = (bf16[24,512]{1,0:T(8,128)(2,1)S(1)}, bf16[24,512]{1,0:T(8,128)(2,1)S(1)}, u32[]{:S(2)}, u32[]{:S(2)}) collective-permute-start(bf16[24,512]{1,0:T(8,128)(2,1)S(1)} %convert.14), channel_id=1, source_target_pairs={{0,80},{16,96},{32,112},{48,128},{64,144},{80,160},{96,176},{112,1... | collective-permute-start | bytes 73736
  277.3 8.1 %collective-permute-start.5 = (bf16[24,512]{1,0:T(8,128)(2,1)S(1)}, bf16[24,512]{1,0:T(8,128)(2,1)S(1)}, u32[]{:S(2)}, u32[]{:S(2)}) collective-permute-start(bf16[24,512]{1,0:T(8,128)(2,1)S(1)} %convert.14), channel_id=1, source_target_pairs={{0,96},{16,112},{32,128},{48,144},{64,160},{80,176},{96,192},{112,... | collective-permute-start | bytes 73736
  280.3 7.8 %collective-permute-start.6 = (bf16[24,512]{1,0:T(8,128)(2,1)S(1)}, bf16[24,512]{1,0:T(8,128)(2,1)S(1)}, u32[]{:S(2)}, u32[]{:S(2)}) collective-permute-start(bf16[24,512]{1,0:T(8,128)(2,1)S(1)} %convert.14), channel_id=1, source_target_pairs={{0,112},{16,128},{32,144},{48,160},{64,176},{80,192},{96,208},{112... | collective-permute-start | bytes 73736
Sparse Core Ops, SparseCore 0:
  43.4 128.2 all-reduce.3
